TPU v7x, 32 devices: a whole 2x2x4 slice. The times are simulated.
32 devices in a mesh: grp: 4 (over y, x), seq: 4 (over z), mlp: 2 (over core).
Axes of the slice: x: 2, y: 2, z: 4, core: 2. Of those that a mesh axis runs over, the one named last changes fastest.
Arguments:
- queries: bfloat16 [16, 4, 4096], P('grp'), may hold values from -6 to 6
- new_keys: bfloat16 [16, 4, 4096], P(('grp', 'seq')), may hold values from -6 to 6
- new_values: bfloat16 [16, 4, 4096], P(('grp', 'seq')), may hold values from -6 to 6
- prefix_keys: bfloat16 [4, 2048, 4096], P('grp', ('seq', 'mlp')), may hold values from -250 to 250
- prefix_values: bfloat16 [4, 2048, 4096], P('grp', ('seq', 'mlp')), may hold values from -6 to 6
- tail_keys: bfloat16 [16, 256, 4096], P(('grp', 'seq'), 'mlp'), may hold values from -6 to 6
- tail_values: bfloat16 [16, 256, 4096], P(('grp', 'seq'), 'mlp'), may hold values from -6 to 6
- prefix_len: int32 [4], P('grp'), may hold values from 1 to 2048, as said below
- tail_len: int32 [16], P('grp'), may hold values from 0 to 256, as said below
- resid: bfloat16 [16, 4, 4096], P('grp', None, ('seq', 'mlp')), may hold values from -12 to 12
- w_out: bfloat16 [4096, 4096], P(None, ('seq', 'mlp')), may hold values from -0.09375 to 0.09375
- ln_gain: bfloat16 [4096], P(('seq', 'mlp')), may hold values from 0.25 to 1.75
- w_up: bfloat16 [4096, 16384], P(('seq', 'mlp'), 'grp'), may hold values from -0.09375 to 0.09375
- w_down: bfloat16 [16384, 4096], P('grp', ('seq', 'mlp')), may hold values from -0.046875 to 0.046875
Outputs:
- out: float32 [16, 4, 4096], P('grp', None, ('seq', 'mlp'))
Inputs may be any that keep to these rules, and one draw needn't show every extreme that they name: `prefix_len`: every group's live prefix is 1 to 2048 slots; in every draw some group's prefix fills all 2048 slots. `tail_len`: A request's live tail is 0 to 256 slots; in every draw some request's tail fills all 256 slots.
All inputs are finite; a program needn't handle non-finite values.
Results may differ from a plain program's by a relative error of at most 0.0075.
Values may be sent and summed in bfloat16 or wider, within the bound.
A program may use at most 128 MiB of HBM per device.

v0:
```python
import math

import jax
import jax.numpy as jnp
from jax import lax
from jax.sharding import PartitionSpec as P

D = 4096
H = 32


NEG = -1e30


def merged(value, axis, join):
    pieces = jax.tree.map(lambda part: lax.all_gather(part, axis), value)
    head = jax.tree.map(lambda part: part[0], pieces)
    tail = jax.tree.map(lambda part: part[1:], pieces)
    so_far, _ = lax.scan(lambda so_far, piece: (join(so_far, piece), None), head, tail)
    return so_far


def head_slopes(count):
    return jnp.power(2.0, -8.0 * (jnp.arange(count, dtype=jnp.float32) + 1.0) / count)


def attend(query_rows, key_block, value_block, query_pos, key_pos, key_mask):
    head_count = query_rows.shape[1]
    inv_scale = 1.0 / math.sqrt(query_rows.shape[2])
    scores = (
        jnp.einsum("qhd,khd->hqk", query_rows, key_block, preferred_element_type=jnp.float32)
        * inv_scale
    )
    distance = (query_pos[:, None] - key_pos[None, :]).astype(jnp.float32)
    scores = scores - head_slopes(head_count)[:, None, None] * distance[None, :, :]
    scores = jnp.where(key_mask, scores, NEG)
    row_max = jnp.max(scores, axis=2)
    weights = jnp.where(key_mask, jnp.exp(scores - row_max[:, :, None]), 0.0)
    weight_sum = jnp.sum(weights, axis=2)
    mixed_sum = jnp.einsum(
        "hqk,khd->qhd",
        weights.astype(jnp.bfloat16),
        value_block,
        preferred_element_type=jnp.float32,
    )
    return (row_max.T, weight_sum.T, mixed_sum)


def join_parts(first, second):
    best_max = jnp.maximum(first[0], second[0])
    factor_one = jnp.exp(first[0] - best_max)
    factor_two = jnp.exp(second[0] - best_max)
    return (
        best_max,
        first[1] * factor_one + second[1] * factor_two,
        first[2] * factor_one[:, :, None] + second[2] * factor_two[:, :, None],
    )


def body(
    queries,
    new_keys,
    new_values,
    prefix_keys,
    prefix_values,
    tail_keys,
    tail_values,
    prefix_len,
    tail_len,
    resid,
    w_out,
    ln_gain,
    w_up,
    w_down,
):
    group_req, step_count, model_width = queries.shape
    head_dim = model_width // H
    row_count = group_req * step_count
    seq_index = lax.axis_index("seq")
    core_index = lax.axis_index("mlp")
    block_len = prefix_keys.shape[1]
    tail_block = tail_keys.shape[1]
    block_start = (seq_index * lax.axis_size("mlp") + core_index) * block_len
    prefix_end = prefix_len[0]
    step_index = jnp.arange(step_count, dtype=jnp.int32)
    query_pos = prefix_end + jnp.repeat(tail_len, step_count) + jnp.tile(step_index, group_req)
    query_rows = queries.reshape(row_count, H, head_dim)
    key_pos = block_start + jnp.arange(block_len, dtype=jnp.int32)
    key_live = key_pos < prefix_end
    own_len = lax.dynamic_index_in_dim(tail_len, seq_index, 0, keepdims=False)
    own_rows = lax.dynamic_slice_in_dim(query_rows, seq_index * step_count, step_count, 0)
    own_pos = prefix_end + own_len + step_index
    tail_index = core_index * tail_block + jnp.arange(tail_block, dtype=jnp.int32)
    partial_value = attend(
        query_rows,
        prefix_keys[0].reshape(block_len, H, head_dim),
        prefix_values[0].reshape(block_len, H, head_dim),
        query_pos,
        key_pos,
        key_live[None, None, :],
    )
    tail_result = attend(
        own_rows,
        tail_keys[0].reshape(tail_block, H, head_dim),
        tail_values[0].reshape(tail_block, H, head_dim),
        own_pos,
        prefix_end + tail_index,
        (tail_index < own_len)[None, None, :],
    )
    self_mask = (step_index[None, :] <= step_index[:, None]) & (core_index == 0)
    self_result = attend(
        own_rows,
        new_keys[0].reshape(step_count, H, head_dim),
        new_values[0].reshape(step_count, H, head_dim),
        own_pos,
        own_pos,
        self_mask[None, :, :],
    )
    own_slice = tuple(
        (
            lax.dynamic_slice_in_dim(member, seq_index * step_count, step_count, 0)
            for member in partial_value
        )
    )
    own_part = join_parts(join_parts(own_slice, tail_result), self_result)
    partial_value = tuple(
        (
            lax.dynamic_update_slice_in_dim(member, update, seq_index * step_count, 0)
            for member, update in zip(partial_value, own_part)
        )
    )
    row_max, weight_sum, mixed_sum = merged(
        (partial_value[0], partial_value[1], partial_value[2]), ("seq", "mlp"), join_parts
    )
    attention = (
        (mixed_sum / weight_sum[:, :, None]).astype(jnp.bfloat16).reshape(row_count, model_width)
    )
    width_block = resid.shape[2]
    stream = resid.astype(jnp.float32).reshape(row_count, width_block) + jnp.dot(
        attention, w_out, preferred_element_type=jnp.float32
    )
    row_sums, squares = lax.psum(
        (jnp.sum(stream, axis=1), jnp.sum(stream * stream, axis=1)), ("seq", "mlp")
    )
    row_mean = row_sums / D
    row_var = squares / D - row_mean * row_mean
    hidden = (
        (stream - row_mean[:, None])
        * lax.rsqrt(row_var[:, None] + 1e-05)
        * ln_gain.astype(jnp.float32)
    ).astype(jnp.bfloat16)
    lifted = jnp.dot(
        lax.all_gather(hidden, "grp", axis=0, tiled=True), w_up, preferred_element_type=jnp.float32
    )
    summed = lax.psum(lifted, ("seq", "mlp"))
    activated = jax.nn.gelu(summed, approximate=False).astype(jnp.bfloat16)
    projected = lax.psum_scatter(
        jnp.dot(activated, w_down, preferred_element_type=jnp.float32),
        "grp",
        scatter_dimension=0,
        tiled=True,
    )
    return (stream + projected).reshape(group_req, step_count, width_block)


def solution(mesh):
    return jax.shard_map(
        body,
        mesh=mesh,
        in_specs=(
            P("grp", None, None),
            P(("grp", "seq"), None, None),
            P(("grp", "seq"), None, None),
            P("grp", ("seq", "mlp"), None),
            P("grp", ("seq", "mlp"), None),
            P(("grp", "seq"), "mlp", None),
            P(("grp", "seq"), "mlp", None),
            P("grp"),
            P("grp"),
            P("grp", None, ("seq", "mlp")),
            P(None, ("seq", "mlp")),
            P(("seq", "mlp")),
            P(("seq", "mlp"), "grp"),
            P("grp", ("seq", "mlp")),
        ),
        out_specs=P("grp", None, ("seq", "mlp")),
        check_vma=False,
    )
```

profile of v0, /device:TPU:0, one launch (start us, length us, event | category | flops | bytes accessed | tf_op | source)
XLA Modules:
  0.0 181.5 jit_solution(5606925134826433128)
XLA Ops:
  7.4 1.2 dynamic_slice.28
  9.2 0.6 fusion.102
  9.8 0.1 subtract_convert_fusion.1
  9.8 0.1 subtract_convert_fusion.2
  9.9 1.1 reshape.182
  11.0 1.4 copy.98
  12.5 0.7 fusion.143
  13.2 0.1 copy.70
  13.3 0.2 fusion.78
  13.5 0.1 copy.78
  13.6 0.1 iota_add_fusion
  13.7 0.1 add.152
  13.8 0.5 copy.97
  14.3 0.1 subtract_convert_fusion
  14.4 1.2 fusion.142
  15.6 0.3 fusion.70
  15.8 0.1 constant_dynamic-slice_fusion
  15.9 0.1 copy.95
  16.0 0.1 copy.96
  16.1 0.2 fusion.81
  16.3 0.1 copy.72
  16.4 0.1 fusion.135
  16.5 0.1 fusion.88
  16.6 0.1 copy.85
  16.7 0.1 copy.87
  16.8 0.1 copy.88
  16.9 0.5 copy.99
  17.4 1.0 fusion.3
  18.4 0.2 copy-done.3
  18.6 0.2 copy.100
  18.9 0.1 copy.91
  18.9 0.1 copy.89
  19.1 0.5 fusion.22
  19.6 0.2 fusion.19
  19.8 0.8 copy.92
  20.7 0.1 copy.82
  20.8 0.2 dynamic_update_slice.13
  21.0 0.1 copy.83
  21.0 15.8 %all_gather.32 = f32[8,16,32]{2,1,0:T(8,128)S(1)} all-gather(f32[1,16,32]{2,1,0:T(8,128)S(1)} %copy.83), channel_id=1, replica_groups=mesh['grp'=4,'seq'=4,'mlp'=2] {'seq','mlp'}, dimensions={0}, use_global_device_ids=true | all-gather | bytes 18432 | tf_op jit(solution)/shard_map/all_gather | solution.py:16
  36.9 0.1 copy.75
  37.0 0.2 dynamic_update_slice.12
  37.2 14.1 %all_gather.29 = f32[8,16,32]{2,1,0:T(8,128)S(1)} all-gather(f32[1,16,32]{2,1,0:T(8,128)S(1)} %copy.76), channel_id=1, replica_groups=mesh['grp'=4,'seq'=4,'mlp'=2] {'seq','mlp'}, dimensions={0}, use_global_device_ids=true | all-gather | bytes 18432 | tf_op jit(solution)/shard_map/all_gather | solution.py:16
  51.4 1.7 all-gather.2.cloned.1.call-done
  53.1 1.7 slice.29
  54.8 1.0 slice_bitcast_fusion
  55.8 2.2 %while.14 = (s32[]{:T(128)}, f32[16,32]{1,0:T(8,128)S(1)}, f32[16,32]{1,0:T(8,128)S(1)}, f32[16,32,128]{2,1,0:T(8,128)S(1)}, f32[7,16,32]{2,1,0:T(8,128)S(1)}, /...) while((s32[]{:T(128)}, f32[16,32]{1,0:T(8,128)S(1)}, f32[16,32]{1,0:T(8,128)S(1)}, ...), condition=%wide.region_7.8_spmd, body=%wide.region_6.7_spmd.sunk | while | flops 199682 | bytes 807005 | solution.py:19
  55.8 0.3 fusion.153
  56.1 0.3 fusion.153
  56.4 0.3 fusion.153
  56.8 0.3 fusion.153
  57.1 0.3 fusion.153
  57.4 0.3 fusion.153
  57.7 0.3 fusion.153
  58.0 0.1 divide_convert_fusion
  58.1 3.0 %fusion.137 = (f32[16]{0:T(128)S(1)}, f32[16]{0:T(128)S(1)}, f32[16,512]{1,0:T(8,128)S(1)}) fusion(f32[16,512]{1,0:T(8,128)S(1)} %reshape.186, bf16[4096,512]{1,0:T(8,128)(2,1)} %param.26, bf16[2,8,32,128]{3,2,1,0:T(8,128)(2,1)S(1)} %bitcast.177), kind=kOutput, calls=%fused_computation.181 | convolution fusion | flops 67141600 | bytes 4391040 | tf_op jit(solution)/shard_map/dot_general | solution.py:139
  61.1 15.5 %all-reduce = (f32[16]{0:T(128)S(1)}, f32[16]{0:T(128)S(1)}) all-reduce(f32[16]{0:T(128)S(1)} %get-tuple-element.60, f32[16]{0:T(128)S(1)} %get-tuple-element.59), channel_id=1, replica_groups=mesh['grp'=4,'seq'=4,'mlp'=2] {'seq','mlp'}, use_global_device_ids=true, to_apply=%region_11.12 | all-reduce | flops 32 | bytes 256 | tf_op jit(solution)/shard_map/psum | solution.py:142
  76.5 0.1 multiply_convert_fusion
  76.6 8.1 %all_gather.36 = bf16[64,512]{1,0:T(8,128)(2,1)S(1)} all-gather(bf16[16,512]{1,0:T(8,128)(2,1)S(1)} %multiply_convert_fusion), channel_id=1, replica_groups=mesh['grp'=4,'seq'=4,'mlp'=2] {'grp'}, dimensions={0}, use_global_device_ids=true | all-gather | bytes 81920 | tf_op jit(solution)/shard_map/all_gather | solution.py:153
  84.8 4.1 %fusion.144 = f32[64,4096]{1,0:T(8,128)} fusion(bf16[64,512]{1,0:T(8,128)(2,1)S(1)} %all_gather.36, bf16[512,4096]{1,0:T(8,128)(2,1)} %param.28), kind=kOutput, calls=%fused_computation.184 | convolution fusion | flops 268435456 | bytes 5308416 | tf_op jit(solution)/shard_map/dot_general | solution.py:152
  88.9 56.1 %all-reduce.3.cloned.1.call-done = f32[64,4096]{1,0:T(8,128)} async-done(((f32[64,4096]{1,0:T(8,128)}), f32[64,4096]{1,0:T(8,128)}) %all-reduce.3.cloned.1.call-update) | async-done | bytes 1048592 | tf_op jit(solution)/shard_map/psum | solution.py:155
  145.1 5.5 %fusion.37 = f32[64,512]{1,0:T(8,128)} fusion(bf16[4096,512]{1,0:T(8,128)(2,1)} %param.29, f32[64,4096]{1,0:T(8,128)} %all-reduce.3.cloned.1.call-done), kind=kOutput, calls=%fused_computation.49 | convolution fusion | flops 285474816 | bytes 5373952 | tf_op jit(solution)/shard_map/dot_general | solution.py:158
  150.6 22.9 %reduce-scatter.2.cloned.1.call-done = f32[16,512]{1,0:T(8,128)} async-done(((f32[64,512]{1,0:T(8,128)}), f32[16,512]{1,0:T(8,128)}) %reduce-scatter.2.cloned.1.call-update) | async-done | bytes 32784 | tf_op jit(solution)/shard_map/reduce_scatter | solution.py:157
  173.6 0.8 add.168
  174.3 0.6 reshape.184
  (45 shorter events, 0.5 us)
Async XLA Ops:
  6.5 13.1 %copy-start = (bf16[1,4,4096]{2,1,0:T(4,128)(2,1)S(1)}, bf16[1,4,4096]{2,1,0:T(4,128)(2,1)}, u32[]{:S(2)}) copy-start(bf16[1,4,4096]{2,1,0:T(4,128)(2,1)} %param.18) | copy-start | bytes 98308
  6.5 7.1 %copy-start.7 = (s32[4]{0:T(128)S(1)}, s32[4]{0:T(128)}, u32[]{:S(2)}) copy-start(s32[4]{0:T(128)} %param.24) | copy-start | bytes 52
  6.5 7.2 %copy-start.1 = (bf16[1,256,4096]{2,1,0:T(8,128)(2,1)S(1)}, bf16[1,256,4096]{2,1,0:T(8,128)(2,1)}, u32[]{:S(2)}) copy-start(bf16[1,256,4096]{2,1,0:T(8,128)(2,1)} %param.19) | copy-start | bytes 6291460
  6.5 46.6 %all-gather.2.cloned.1.call-start = ((), (), s32[]{:S(2)}) async-start(), calls=%async_computation.1 | async-start | bytes 2359296 | tf_op jit(solution)/shard_map/all_gather | solution.py:16
  14.3 1.8 copy-start.4
  14.3 2.6 %copy-start.2 = (bf16[1,256,4096]{2,1,0:T(8,128)(2,1)S(1)}, bf16[1,256,4096]{2,1,0:T(8,128)(2,1)}, u32[]{:S(2)}) copy-start(bf16[1,256,4096]{2,1,0:T(8,128)(2,1)} %param.20) | copy-start | bytes 6291460
  17.3 1.2 copy-start.3
  18.8 32.5 %copy-start.5 = (bf16[4,4,512]{2,1,0:T(4,128)(2,1)S(1)}, bf16[4,4,512]{2,1,0:T(4,128)(2,1)}, u32[]{:S(2)}) copy-start(bf16[4,4,512]{2,1,0:T(4,128)(2,1)} %param.25) | copy-start | bytes 49156
  18.8 32.5 %copy-start.6 = (bf16[512]{0:T(512)(128)(2,1)S(1)}, bf16[512]{0:T(512)(128)(2,1)}, u32[]{:S(2)}) copy-start(bf16[512]{0:T(512)(128)(2,1)} %param.27) | copy-start | bytes 3076
  20.6 124.4 %all-reduce.3.cloned.1.call-start = ((), (), s32[]{:S(2)}) async-start(), calls=%async_computation.2 | async-start | bytes 2097152 | tf_op jit(solution)/shard_map/psum | solution.py:155
  88.9 84.7 %reduce-scatter.2.cloned.1.call-start = ((), (), s32[]{:S(2)}) async-start(), calls=%async_computation.3 | async-start | bytes 163840 | tf_op jit(solution)/shard_map/reduce_scatter | solution.py:157
Sparse Core Ops, SparseCore 0:
  20.8 32.3 all-gather.1
  89.0 56.0 all-reduce.2
  150.7 22.7 reduce-scatter.1
where the time goes:
time: 182 us; the launch traced here: 181 us
  waiting for transfers between devices  80.9 us (44%)
  blocking collectives  53.5 us (29%)
  matrix products  16.5 us (9%)
  between operations  14.8 us (8%)
  local copies, waits for them, and re-layouts  11 us (6%)
  other arithmetic  4.55 us (2%)
    psum x1, waiting for transfers between devices, body(): summed = lax.psum(lifted, ('seq', 'mlp'))  56.1 us
    all_gather x2, blocking collectives, merged(): pieces = jax.tree.map(lambda part: lax.all_gather(part, axis), value)  29.9 us
    reduce_scatter x1, waiting for transfers between devices, body(): lax.psum_scatter(jnp.dot(activated, w_down, preferred_element_type=jnp.fl...  22.9 us
    psum x1, blocking collectives, body(): lax.psum((jnp.sum(stream, axis=1), jnp.sum(stream * stream, axis=1)), ('s...  15.5 us
    all_gather x1, blocking collectives, body(): lax.all_gather(hidden, 'grp', axis=0, tiled=True)  8.13 us
    dot_general x1, matrix products, body(): jnp.dot(activated, w_down, preferred_element_type=jnp.float32)  5.52 us
    dot_general x1, matrix products, body(): jnp.dot(lax.all_gather(hidden, 'grp', axis=0, tiled=True), w_up, preferre...  4.1 us
  transfers between devices with their start and end apart: 3, of which 3 were waited for; matrix products, arithmetic and copies ran while one was open for 0% of the time, Pallas kernels for 0%

commit v1 on v0

--- a/solution.py
+++ b/solution.py
@@ -1,8 +1,12 @@
+import functools
 import math
 
 import jax
 import jax.numpy as jnp
+import numpy as np
 from jax import lax
+from jax.experimental import pallas as pl
+from jax.experimental.pallas import tpu as pltpu
 from jax.sharding import PartitionSpec as P
 
 D = 4096
@@ -163,9 +167,537 @@
     return (stream + projected).reshape(group_req, step_count, width_block)
 
 
+F32 = jnp.float32
+BF16 = jnp.bfloat16
+LANES = 128
+NEW_PAD = 16
+FLOOR = -1e29
+FAR = 1e33
+
+
+def remote(src, dst, send_sem, recv_sem, device):
+    return pltpu.make_async_remote_copy(
+        src_ref=src,
+        dst_ref=dst,
+        send_sem=send_sem,
+        recv_sem=recv_sem,
+        device_id=device,
+        device_id_type=pl.DeviceIdType.MESH,
+    )
+
+
+def layer_kernel(
+    G,
+    S,
+    C,
+    q_hbm,
+    nk_hbm,
+    nv_hbm,
+    pk_hbm,
+    pv_hbm,
+    tk_hbm,
+    tv_hbm,
+    plen,
+    tlen,
+    slopes,
+    resid_hbm,
+    gain_ref,
+    wo_hbm,
+    wu_hbm,
+    wd_hbm,
+    out_ref,
+    q_in,
+    nk_in,
+    nv_in,
+    resid_in,
+    stage,
+    qbuf,
+    kbuf,
+    vbuf,
+    dist,
+    wo,
+    wu,
+    wd,
+    o_send,
+    o_recv,
+    st_send,
+    st_recv,
+    att,
+    ybuf,
+    sum_send,
+    sum_recv,
+    hid,
+    up_send,
+    up_pair,
+    up_zsend,
+    up_zrecv,
+    act,
+    acc,
+    proj_send,
+    proj_recv,
+    load_sem,
+    o_ss,
+    o_rs,
+    st_ss,
+    st_rs,
+    att_ss,
+    att_rs,
+    sum_ss,
+    sum_rs,
+    hid_ss,
+    hid_rs,
+    pair_ss,
+    pair_rs,
+    zup_ss,
+    zup_rs,
+    act_ss,
+    fwd_ss,
+    act_rs,
+    proj_ss,
+    proj_rs,
+):
+    N = S * C
+    grp = lax.axis_index("grp")
+    seq = lax.axis_index("seq")
+    core = lax.axis_index("mlp")
+    me = seq * C + core
+    group_req, steps, width = q_in.shape
+    rows = group_req * steps
+    prefix = pk_hbm.shape[1]
+    tail = tk_hbm.shape[1]
+    keys = kbuf.shape[0]
+    block = ybuf.shape[1]
+    head_dim = width // H
+    heads = block // head_dim
+
+    def peer(index):
+        return {"seq": index // C, "mlp": lax.rem(index, C)}
+
+    loads = [
+        pltpu.make_async_copy(q_hbm, q_in, load_sem.at[0]),
+        pltpu.make_async_copy(nk_hbm, nk_in, load_sem.at[1]),
+        pltpu.make_async_copy(nv_hbm, nv_in, load_sem.at[2]),
+        pltpu.make_async_copy(pk_hbm.at[0], kbuf.at[pl.ds(0, prefix)], load_sem.at[3]),
+        pltpu.make_async_copy(tk_hbm.at[0], kbuf.at[pl.ds(prefix, tail)], load_sem.at[4]),
+        pltpu.make_async_copy(pv_hbm.at[0], vbuf.at[pl.ds(0, prefix)], load_sem.at[5]),
+        pltpu.make_async_copy(tv_hbm.at[0], vbuf.at[pl.ds(prefix, tail)], load_sem.at[6]),
+        pltpu.make_async_copy(resid_hbm, resid_in, load_sem.at[7]),
+    ]
+    wo_load = pltpu.make_async_copy(wo_hbm, wo, load_sem.at[8])
+    wu_load = pltpu.make_async_copy(wu_hbm, wu, load_sem.at[9])
+    wd_load = pltpu.make_async_copy(wd_hbm, wd, load_sem.at[10])
+    for load in loads:
+        load.start()
+
+    barrier = pltpu.get_barrier_semaphore()
+    for k in range(1, N):
+        pl.semaphore_signal(
+            barrier, inc=1, device_id=peer(lax.rem(me + k, N)), device_id_type=pl.DeviceIdType.MESH
+        )
+    for k in range(1, G):
+        pl.semaphore_signal(
+            barrier,
+            inc=1,
+            device_id={"grp": lax.rem(grp + k, G)},
+            device_id_type=pl.DeviceIdType.MESH,
+        )
+
+    row = lax.broadcasted_iota(jnp.int32, (rows, keys), 0)
+    col = lax.broadcasted_iota(jnp.int32, (rows, keys), 1)
+    request = row // steps
+    step = row - request * steps
+    prefix_end = plen[0]
+    length = jnp.zeros((rows, keys), jnp.int32)
+    for r in range(group_req):
+        length = jnp.where(request == r, tlen[r], length)
+    own = request == seq
+    key_pos = me * prefix + col
+    tail_pos = core * tail + col - prefix
+    new_pos = col - prefix - tail
+    is_prefix = col < prefix
+    is_tail = jnp.logical_and(col >= prefix, col < prefix + tail)
+    is_new = jnp.logical_and(col >= prefix + tail, new_pos < steps)
+    apart = jnp.where(
+        is_prefix,
+        prefix_end + length + step - key_pos,
+        jnp.where(is_tail, length + step - tail_pos, step - new_pos),
+    )
+    live_prefix = jnp.logical_and(is_prefix, key_pos < prefix_end)
+    live_tail = jnp.logical_and(jnp.logical_and(is_tail, tail_pos < length), own)
+    live_new = jnp.logical_and(
+        jnp.logical_and(is_new, new_pos <= step), jnp.logical_and(own, core == 0)
+    )
+    live = jnp.logical_or(live_prefix, jnp.logical_or(live_tail, live_new))
+    dist[...] = jnp.where(live, apart.astype(F32), FAR)
+
+    stage[...] = jnp.zeros_like(stage)
+    loads[1].wait()
+    stage[0:steps, :] = nk_in[0].astype(F32)
+    kbuf[prefix + tail : keys, :] = stage[...].astype(BF16)
+    loads[2].wait()
+    stage[0:steps, :] = nv_in[0].astype(F32)
+    vbuf[prefix + tail : keys, :] = stage[...].astype(BF16)
+    loads[0].wait()
+    for r in range(group_req):
+        stage[r * steps : (r + 1) * steps, :] = q_in[r].astype(F32)
+    qbuf[...] = stage[...].astype(BF16)
+    loads[7].wait()
+    for r in range(group_req):
+        ybuf[r * steps : (r + 1) * steps, :] = resid_in[r].astype(F32)
+
+    for i in range(3, 7):
+        loads[i].wait()
+    wo_load.start()
+    wu_load.start()
+    wd_load.start()
+
+    pl.semaphore_wait(barrier, N - 1 + G - 1)
+
+    inv_scale = 1.0 / math.sqrt(head_dim)
+    lane = lax.broadcasted_iota(jnp.int32, (rows, LANES), 1)
+
+    def partials(i, carry):
+        p = lax.rem(me + 1 + i, N)
+        base = pl.multiple_of(p * block, block)
+        stats = jnp.zeros((rows, LANES), F32)
+        for j in range(heads):
+            cols = pl.ds(base + j * head_dim, head_dim)
+            scores = lax.dot_general(
+                qbuf[:, cols], kbuf[:, cols], (((1,), (1,)), ((), ())), preferred_element_type=F32
+            )
+            scores = scores * inv_scale - slopes[p * heads + j] * dist[...]
+            top = jnp.maximum(jnp.max(scores, axis=1, keepdims=True), FLOOR)
+            weights = jnp.exp(scores - top)
+            total = jnp.sum(weights, axis=1, keepdims=True)
+            mixed = jnp.dot(weights.astype(BF16), vbuf[:, cols], preferred_element_type=F32)
+            o_send[p, :, j * head_dim : (j + 1) * head_dim] = mixed.astype(BF16)
+            stats = jnp.where(lane == j, top, stats)
+            stats = jnp.where(lane == heads + j, total, stats)
+        st_send[p] = stats
+
+        @pl.when(i < N - 1)
+        def _():
+            remote(o_send.at[p], o_recv.at[me], o_ss.at[p], o_rs.at[me], peer(p)).start()
+            remote(st_send.at[p], st_recv.at[me], st_ss.at[p], st_rs.at[me], peer(p)).start()
+
+        return carry
+
+    lax.fori_loop(0, N, partials, 0)
+    o_recv[me] = o_send[me]
+    st_recv[me] = st_send[me]
+
+    for k in range(1, N):
+        p = lax.rem(me + N - k, N)
+        remote(o_send.at[p], o_recv.at[p], o_ss.at[p], o_rs.at[p], peer(p)).wait_recv()
+        remote(st_send.at[p], st_recv.at[p], st_ss.at[p], st_rs.at[p], peer(p)).wait_recv()
+    stats = [st_recv[i] for i in range(N)]
+    best = stats[0]
+    for i in range(1, N):
+        best = jnp.maximum(best, stats[i])
+    factors = [jnp.exp(member - best) for member in stats]
+    whole = factors[0] * pltpu.roll(stats[0], LANES - heads, 1)
+    for i in range(1, N):
+        whole = whole + factors[i] * pltpu.roll(stats[i], LANES - heads, 1)
+    for j in range(heads):
+        cols = slice(j * head_dim, (j + 1) * head_dim)
+        mixed = o_recv[0, :, cols].astype(F32) * factors[0][:, j : j + 1]
+        for i in range(1, N):
+            mixed = mixed + o_recv[i, :, cols].astype(F32) * factors[i][:, j : j + 1]
+        att[me, :, cols] = (mixed / whole[:, j : j + 1]).astype(BF16)
+    for k in range(1, N):
+        p = lax.rem(me + k, N)
+        remote(att.at[me], att.at[me], att_ss.at[p], att_rs.at[me], peer(p)).start()
+
+    wo_load.wait()
+
+    def out_proj(k, carry):
+        p = lax.rem(me + N - k, N)
+
+        @pl.when(k > 0)
+        def _():
+            remote(att.at[p], att.at[p], att_ss.at[p], att_rs.at[p], peer(p)).wait_recv()
+
+        piece = pl.ds(pl.multiple_of(p * block, block), block)
+        ybuf[...] += jnp.dot(att[p], wo[piece, :], preferred_element_type=F32)
+        return carry
+
+    lax.fori_loop(0, N, out_proj, 0)
+
+    y = ybuf[...]
+    sums = jnp.where(lane == 0, jnp.sum(y, axis=1, keepdims=True), 0.0)
+    sums = jnp.where(lane == 1, jnp.sum(y * y, axis=1, keepdims=True), sums)
+    sum_send[...] = sums
+    for k in range(1, N):
+        p = lax.rem(me + k, N)
+        remote(sum_send, sum_recv.at[me], sum_ss.at[p], sum_rs.at[me], peer(p)).start()
+    sum_recv[me] = sums
+    for k in range(1, N):
+        p = lax.rem(me + N - k, N)
+        remote(sum_send, sum_recv.at[p], sum_ss.at[p], sum_rs.at[p], peer(p)).wait_recv()
+    sums = jnp.sum(sum_recv[...], axis=0)
+    mean = sums[:, 0:1] / width
+    var = sums[:, 1:2] / width - mean * mean
+    hidden = (y - mean) * lax.rsqrt(var + 1e-05) * gain_ref[...].astype(F32)
+    mine = pl.ds(pl.multiple_of(grp * rows, rows), rows)
+    hid[mine, :] = hidden.astype(BF16)
+    for k in range(1, G):
+        g = lax.rem(grp + k, G)
+        remote(hid.at[mine], hid.at[mine], hid_ss.at[g], hid_rs.at[grp], {"grp": g}).start()
+    wu_load.wait()
+    for k in range(1, G):
+        g = lax.rem(grp + G - k, G)
+        theirs = pl.ds(pl.multiple_of(g * rows, rows), rows)
+        remote(hid.at[theirs], hid.at[theirs], hid_ss.at[g], hid_rs.at[g], {"grp": g}).wait_recv()
+
+    other = 1 - core
+
+    def lift(index):
+        piece = pl.ds(pl.multiple_of(index * act.shape[2], act.shape[2]), act.shape[2])
+        return jnp.dot(hid[...], wu[:, piece], preferred_element_type=F32)
+
+    def pair_blocks(k, carry):
+        z = lax.rem(seq + 1 + k, S)
+        up_send[z] = lift(z * C + other).astype(BF16)
+        remote(up_send.at[z], up_pair.at[z], pair_ss.at[z], pair_rs.at[z], {"mlp": other}).start()
+        return carry
+
+    lax.fori_loop(0, S, pair_blocks, 0)
+
+    def z_blocks(k, carry):
+        z = lax.rem(seq + 1 + k, S)
+        part = lift(z * C + core)
+        remote(
+            up_send.at[z], up_pair.at[z], pair_ss.at[z], pair_rs.at[z], {"mlp": other}
+        ).wait_recv()
+        part = part + up_pair[z].astype(F32)
+
+        @pl.when(k < S - 1)
+        def _():
+            up_zsend[z] = part.astype(BF16)
+            remote(
+                up_zsend.at[z], up_zrecv.at[seq], zup_ss.at[z], zup_rs.at[seq], {"seq": z}
+            ).start()
+
+        @pl.when(k == S - 1)
+        def _():
+            acc[...] = part
+
+        return carry
+
+    lax.fori_loop(0, S, z_blocks, 0)
+    lifted = acc[...]
+    for k in range(1, S):
+        z = lax.rem(seq + S - k, S)
+        remote(
+            up_zsend.at[z], up_zrecv.at[z], zup_ss.at[z], zup_rs.at[z], {"seq": z}
+        ).wait_recv()
+        lifted = lifted + up_zrecv[z].astype(F32)
+    act[me] = (0.5 * lifted * (1.0 + lax.erf(lifted * math.sqrt(0.5)))).astype(BF16)
+
+    for k in range(1, S):
+        z = lax.rem(seq + k, S)
+        remote(act.at[me], act.at[me], act_ss.at[z], act_rs.at[me], {"seq": z}).start()
+    remote(act.at[me], act.at[me], fwd_ss.at[seq], act_rs.at[me], {"mlp": other}).start()
+
+    wd_load.wait()
+
+    def lower(index):
+        piece = pl.ds(pl.multiple_of(index * act.shape[2], act.shape[2]), act.shape[2])
+        return jnp.dot(act[index], wd[piece, :], preferred_element_type=F32)
+
+    acc[...] = lower(me)
+
+    def down(k, carry):
+        z = lax.rem(seq + S - k, S)
+        near = z * C + core
+        far = z * C + other
+
+        @pl.when(k > 0)
+        def _():
+            remote(act.at[near], act.at[near], act_ss.at[z], act_rs.at[near], {"seq": z}).wait_recv()
+            remote(act.at[near], act.at[near], fwd_ss.at[z], act_rs.at[near], {"mlp": other}).start()
+            acc[...] += lower(near)
+
+        remote(act.at[far], act.at[far], fwd_ss.at[z], act_rs.at[far], {"mlp": other}).wait_recv()
+        acc[...] += lower(far)
+        return carry
+
+    lax.fori_loop(0, S, down, 0)
+
+    for k in range(1, G):
+        g = lax.rem(grp + k, G)
+        theirs = pl.ds(pl.multiple_of(g * rows, rows), rows)
+        proj_send[g] = acc[theirs, :].astype(BF16)
+        remote(
+            proj_send.at[g], proj_recv.at[grp], proj_ss.at[g], proj_rs.at[grp], {"grp": g}
+        ).start()
+    total = ybuf[...] + acc[mine, :]
+    for k in range(1, G):
+        g = lax.rem(grp + G - k, G)
+        remote(
+            proj_send.at[g], proj_recv.at[g], proj_ss.at[g], proj_rs.at[g], {"grp": g}
+        ).wait_recv()
+        total = total + proj_recv[g].astype(F32)
+    ybuf[...] = total
+    for r in range(group_req):
+        out_ref[r] = ybuf[r * steps : (r + 1) * steps, :]
+
+    for k in range(1, N):
+        p = lax.rem(me + k, N)
+        remote(o_send.at[p], o_recv.at[me], o_ss.at[p], o_rs.at[me], peer(p)).wait_send()
+        remote(st_send.at[p], st_recv.at[me], st_ss.at[p], st_rs.at[me], peer(p)).wait_send()
+        remote(att.at[me], att.at[me], att_ss.at[p], att_rs.at[me], peer(p)).wait_send()
+        remote(sum_send, sum_recv.at[me], sum_ss.at[p], sum_rs.at[me], peer(p)).wait_send()
+    for k in range(1, G):
+        g = lax.rem(grp + k, G)
+        remote(hid.at[mine], hid.at[mine], hid_ss.at[g], hid_rs.at[grp], {"grp": g}).wait_send()
+        remote(
+            proj_send.at[g], proj_recv.at[grp], proj_ss.at[g], proj_rs.at[grp], {"grp": g}
+        ).wait_send()
+    for z in range(S):
+        remote(
+            up_send.at[z], up_pair.at[z], pair_ss.at[z], pair_rs.at[z], {"mlp": other}
+        ).wait_send()
+        near = z * C + core
+        remote(act.at[near], act.at[near], fwd_ss.at[z], act_rs.at[near], {"mlp": other}).wait_send()
+    for k in range(1, S):
+        z = lax.rem(seq + k, S)
+        remote(
+            up_zsend.at[z], up_zrecv.at[seq], zup_ss.at[z], zup_rs.at[seq], {"seq": z}
+        ).wait_send()
+        remote(act.at[me], act.at[me], act_ss.at[z], act_rs.at[me], {"seq": z}).wait_send()
+
+
+def fused(
+    G,
+    S,
+    C,
+    queries,
+    new_keys,
+    new_values,
+    prefix_keys,
+    prefix_values,
+    tail_keys,
+    tail_values,
+    prefix_len,
+    tail_len,
+    resid,
+    w_out,
+    ln_gain,
+    w_up,
+    w_down,
+):
+    group_req, steps, width = queries.shape
+    rows = group_req * steps
+    N = S * C
+    block = resid.shape[2]
+    lifted = w_up.shape[1] // N
+    keys = prefix_keys.shape[1] + tail_keys.shape[1] + NEW_PAD
+    slopes = jnp.asarray(np.power(2.0, -8.0 * (np.arange(H) + 1.0) / H).astype(np.float32))
+    dma = pltpu.SemaphoreType.DMA
+    hbm = pl.BlockSpec(memory_space=pl.ANY)
+    smem = pl.BlockSpec(memory_space=pltpu.SMEM)
+    vmem = pl.BlockSpec(memory_space=pltpu.VMEM)
+    return pl.pallas_call(
+        functools.partial(layer_kernel, G, S, C),
+        out_shape=jax.ShapeDtypeStruct((group_req, steps, block), F32),
+        in_specs=[hbm] * 7 + [smem] * 3 + [hbm, vmem] + [hbm] * 3,
+        out_specs=vmem,
+        scratch_shapes=[
+            pltpu.VMEM(queries.shape, BF16),
+            pltpu.VMEM(new_keys.shape, BF16),
+            pltpu.VMEM(new_values.shape, BF16),
+            pltpu.VMEM(resid.shape, BF16),
+            pltpu.VMEM((rows, width), F32),
+            pltpu.VMEM((rows, width), BF16),
+            pltpu.VMEM((keys, width), BF16),
+            pltpu.VMEM((keys, width), BF16),
+            pltpu.VMEM((rows, keys), F32),
+            pltpu.VMEM(w_out.shape, BF16),
+            pltpu.VMEM(w_up.shape, BF16),
+            pltpu.VMEM(w_down.shape, BF16),
+            pltpu.VMEM((N, rows, block), BF16),
+            pltpu.VMEM((N, rows, block), BF16),
+            pltpu.VMEM((N, rows, LANES), F32),
+            pltpu.VMEM((N, rows, LANES), F32),
+            pltpu.VMEM((N, rows, block), BF16),
+            pltpu.VMEM((rows, block), F32),
+            pltpu.VMEM((rows, LANES), F32),
+            pltpu.VMEM((N, rows, LANES), F32),
+            pltpu.VMEM((G * rows, block), BF16),
+            pltpu.VMEM((S, G * rows, lifted), BF16),
+            pltpu.VMEM((S, G * rows, lifted), BF16),
+            pltpu.VMEM((S, G * rows, lifted), BF16),
+            pltpu.VMEM((S, G * rows, lifted), BF16),
+            pltpu.VMEM((N, G * rows, lifted), BF16),
+            pltpu.VMEM((G * rows, block), F32),
+            pltpu.VMEM((G, rows, block), BF16),
+            pltpu.VMEM((G, rows, block), BF16),
+            dma((11,)),
+            dma((N,)),
+            dma((N,)),
+            dma((N,)),
+            dma((N,)),
+            dma((N,)),
+            dma((N,)),
+            dma((N,)),
+            dma((N,)),
+            dma((G,)),
+            dma((G,)),
+            dma((S,)),
+            dma((S,)),
+            dma((S,)),
+            dma((S,)),
+            dma((S,)),
+            dma((S,)),
+            dma((N,)),
+            dma((G,)),
+            dma((G,)),
+        ],
+        compiler_params=pltpu.CompilerParams(
+            collective_id=0, has_side_effects=True, vmem_limit_bytes=44 * 1024 * 1024
+        ),
+        cost_estimate=pl.CostEstimate(
+            flops=2 * rows * width * (keys * 2 + block) + 4 * G * rows * block * w_up.shape[1],
+            bytes_accessed=4 * keys * width + 2 * (w_out.size + w_up.size + w_down.size),
+            transcendentals=rows * keys * H,
+        ),
+    )(
+        queries,
+        new_keys,
+        new_values,
+        prefix_keys,
+        prefix_values,
+        tail_keys,
+        tail_values,
+        prefix_len,
+        tail_len,
+        slopes,
+        resid,
+        ln_gain.reshape(1, block),
+        w_out,
+        w_up,
+        w_down,
+    )
+
+
+def layer_body(mesh):
+    G, S, C = (mesh.shape[axis] for axis in ("grp", "seq", "mlp"))
+
+    def run(*args):
+        rows = args[0].shape[0] * args[0].shape[1]
+        block = args[9].shape[2]
+        lifted = args[12].shape[1] // (S * C)
+        if C == 2 and lifted == block and block % LANES == 0 and rows == NEW_PAD:
+            return fused(G, S, C, *args)
+        return body(*args)
+
+    return run
+
+
 def solution(mesh):
     return jax.shard_map(
-        body,
+        layer_body(mesh),
         mesh=mesh,
         in_specs=(
             P("grp", None, None),

time: 182 us -> 64.6 us (0.35)
  waiting for transfers between devices: 80.9 us -> 0 us
  blocking collectives: 53.5 us -> 0 us
  Pallas kernels: 0 us -> 52.1 us
  matrix products: 16.5 us -> 0 us
  between operations: 14.8 us -> 0.67 us
  other arithmetic: 4.55 us -> 0 us
    psum x1 -> x0, waiting for transfers between devices: 56.1 us -> none  [body(): summed = lax.psum(lifted, ('seq', 'mlp'))]
    pallas_call x0 -> x1, Pallas kernels: none -> 52.1 us  [fused(): pl.pallas_call(functools.partial(layer_kernel, G, S, C), out_shape=jax.Sh...]
    all_gather x3 -> x0, blocking collectives: 38.1 us -> none  [the longest x2 29.9 us: merged(): pieces = jax.tree.map(lambda part: lax.all_gather(part, axis), value)]
    reduce_scatter x1 -> x0, waiting for transfers between devices: 22.9 us -> none  [body(): lax.psum_scatter(jnp.dot(activated, w_down, preferred_element_type=jnp.fl...]
    dot_general x9 -> x0, matrix products: 16.5 us -> none  [the longest x1 5.52 us: body(): jnp.dot(activated, w_down, preferred_element_type=jnp.float32)]
    psum x1 -> x0, blocking collectives: 15.5 us -> none  [body(): lax.psum((jnp.sum(stream, axis=1), jnp.sum(stream * stream, axis=1)), ('s...]
    unnamed x22 -> x21, local copies, waits for them, and re-layouts: 3.01 us -> 10.7 us
    add x20 -> x0, other arithmetic: 2.84 us -> none  [the longest x7 1.84 us: join_parts(): first[2] * factor_one[:, :, None] + second[2] * factor_two[:, :, None]]
  transfers between devices with their start and end apart: 3 -> 0, of which waited for: 3 -> 0; matrix products, arithmetic and copies ran while one was open for 0% -> 0% of each run, Pallas kernels for 0% -> 0%
where the time goes in v1:
time: 64.6 us; the launch traced here: 64.1 us
  Pallas kernels  52.1 us (81%)
  local copies, waits for them, and re-layouts  11.4 us (18%)
  between operations  0.67 us (1%)
    pallas_call x1, Pallas kernels, fused(): pl.pallas_call(functools.partial(layer_kernel, G, S, C), out_shape=jax.Sh...  52.1 us
    unnamed x21, local copies, waits for them, and re-layouts  10.7 us

profile of v1, /device:TPU:0, one launch (start us, length us, event | category | flops | bytes accessed | tf_op | source)
XLA Modules:
  0.0 64.1 jit_solution(7858333550757041833)
XLA Ops:
  0.7 0.7 %reshape.3.gain_ref = bf16[1,512]{1,0:T(2,128)(2,1)S(1)} reshape(bf16[512]{0:T(512)(128)(2,1)} %param.26) | data formatting | bytes 2048 | tf_op jit(solution)/shard_map/reshape | solution.py:677
  1.3 0.0 copy-start
  1.3 1.6 %copy-done = bf16[1,256,4096]{2,1,0:T(8,128)(2,1)S(1)} copy-done((bf16[1,256,4096]{2,1,0:T(8,128)(2,1)S(1)}, bf16[1,256,4096]{2,1,0:T(8,128)(2,1)}, u32[]{:S(2)}) %copy-start) | copy-done | bytes 2097176
  2.9 0.0 copy-start.1
  2.9 1.6 %copy-done.1 = bf16[1,256,4096]{2,1,0:T(8,128)(2,1)S(1)} copy-done((bf16[1,256,4096]{2,1,0:T(8,128)(2,1)S(1)}, bf16[1,256,4096]{2,1,0:T(8,128)(2,1)}, u32[]{:S(2)}) %copy-start.1) | copy-done | bytes 2097176
  4.5 0.0 copy-start.2
  4.5 1.2 %copy-done.2 = bf16[1,128,4096]{2,1,0:T(8,128)(2,1)S(1)} copy-done((bf16[1,128,4096]{2,1,0:T(8,128)(2,1)S(1)}, bf16[1,128,4096]{2,1,0:T(8,128)(2,1)}, u32[]{:S(2)}) %copy-start.2) | copy-done | bytes 1048600
  5.7 0.0 copy-start.3
  5.7 1.2 %copy-done.3 = bf16[1,128,4096]{2,1,0:T(8,128)(2,1)S(1)} copy-done((bf16[1,128,4096]{2,1,0:T(8,128)(2,1)S(1)}, bf16[1,128,4096]{2,1,0:T(8,128)(2,1)}, u32[]{:S(2)}) %copy-start.3) | copy-done | bytes 1048600
  7.0 0.0 copy-start.4
  7.0 0.9 %copy-done.4 = bf16[4,4,4096]{2,1,0:T(4,128)(2,1)S(1)} copy-done((bf16[4,4,4096]{2,1,0:T(4,128)(2,1)S(1)}, bf16[4,4,4096]{2,1,0:T(4,128)(2,1)}, u32[]{:S(2)}) %copy-start.4) | copy-done | bytes 131096
  7.9 0.0 copy-start.5
  7.9 0.8 %copy-done.5 = bf16[1,4,4096]{2,1,0:T(4,128)(2,1)S(1)} copy-done((bf16[1,4,4096]{2,1,0:T(4,128)(2,1)S(1)}, bf16[1,4,4096]{2,1,0:T(4,128)(2,1)}, u32[]{:S(2)}) %copy-start.5) | copy-done | bytes 32792
  8.6 0.0 copy-start.6
  8.6 0.8 %copy-done.6 = bf16[1,4,4096]{2,1,0:T(4,128)(2,1)S(1)} copy-done((bf16[1,4,4096]{2,1,0:T(4,128)(2,1)S(1)}, bf16[1,4,4096]{2,1,0:T(4,128)(2,1)}, u32[]{:S(2)}) %copy-start.6) | copy-done | bytes 32792
  9.4 0.0 copy-start.7
  9.4 0.7 %copy-done.7 = bf16[4,4,512]{2,1,0:T(4,128)(2,1)S(1)} copy-done((bf16[4,4,512]{2,1,0:T(4,128)(2,1)S(1)}, bf16[4,4,512]{2,1,0:T(4,128)(2,1)}, u32[]{:S(2)}) %copy-start.7) | copy-done | bytes 16408
  10.1 0.0 copy-start.8
  10.1 0.7 %copy-done.8 = s32[4]{0:T(128)S(1)} copy-done((s32[4]{0:T(128)S(1)}, s32[4]{0:T(128)}, u32[]{:S(2)}) %copy-start.8) | copy-done | bytes 40
  10.8 0.0 copy-start.9
  10.8 0.7 %copy-done.9 = f32[32]{0:T(128)S(1)} copy-done((f32[32]{0:T(128)S(1)}, f32[32]{0:T(128)}, u32[]{:S(2)}) %copy-start.9) | copy-done | bytes 152
  11.4 52.1 %shard_map.145 = f32[4,4,512]{2,1,0:T(4,128)S(1)} custom-call(bf16[4,4,4096]{2,1,0:T(4,128)(2,1)S(1)} %copy-done.4, bf16[1,4,4096]{2,1,0:T(4,128)(2,1)S(1)} %copy-done.5, bf16[1,4,4096]{2,1,0:T(4,128)(2,1)S(1)} %copy-done.6, bf16[1,256,4096]{2,1,0:T(8,128)(2,1)S(1)} %copy-done, bf16[1,256,4096]{2,1,0:T(8,128)(2,1)S(1)} %copy-done.1, ...), custom_call_target="tpu_custom_call" | custom-call | flops 708837376 | bytes 19136512 | tf_op jit(solution)/shard_map/pallas_call | solution.py:601
  63.5 0.6 copy.18
Async XLA Ops:
  1.3 1.6 %copy-start = (bf16[1,256,4096]{2,1,0:T(8,128)(2,1)S(1)}, bf16[1,256,4096]{2,1,0:T(8,128)(2,1)}, u32[]{:S(2)}) copy-start(bf16[1,256,4096]{2,1,0:T(8,128)(2,1)} %pk_hbm.1) | copy-start | bytes 6291460
  2.9 1.6 %copy-start.1 = (bf16[1,256,4096]{2,1,0:T(8,128)(2,1)S(1)}, bf16[1,256,4096]{2,1,0:T(8,128)(2,1)}, u32[]{:S(2)}) copy-start(bf16[1,256,4096]{2,1,0:T(8,128)(2,1)} %pv_hbm.1) | copy-start | bytes 6291460
  4.5 1.2 %copy-start.2 = (bf16[1,128,4096]{2,1,0:T(8,128)(2,1)S(1)}, bf16[1,128,4096]{2,1,0:T(8,128)(2,1)}, u32[]{:S(2)}) copy-start(bf16[1,128,4096]{2,1,0:T(8,128)(2,1)} %tk_hbm.1) | copy-start | bytes 3145732
  5.7 1.2 %copy-start.3 = (bf16[1,128,4096]{2,1,0:T(8,128)(2,1)S(1)}, bf16[1,128,4096]{2,1,0:T(8,128)(2,1)}, u32[]{:S(2)}) copy-start(bf16[1,128,4096]{2,1,0:T(8,128)(2,1)} %tv_hbm.1) | copy-start | bytes 3145732
  7.0 0.9 %copy-start.4 = (bf16[4,4,4096]{2,1,0:T(4,128)(2,1)S(1)}, bf16[4,4,4096]{2,1,0:T(4,128)(2,1)}, u32[]{:S(2)}) copy-start(bf16[4,4,4096]{2,1,0:T(4,128)(2,1)} %q_hbm.1) | copy-start | bytes 393220
  7.9 0.8 %copy-start.5 = (bf16[1,4,4096]{2,1,0:T(4,128)(2,1)S(1)}, bf16[1,4,4096]{2,1,0:T(4,128)(2,1)}, u32[]{:S(2)}) copy-start(bf16[1,4,4096]{2,1,0:T(4,128)(2,1)} %nk_hbm.1) | copy-start | bytes 98308
  8.6 0.8 %copy-start.6 = (bf16[1,4,4096]{2,1,0:T(4,128)(2,1)S(1)}, bf16[1,4,4096]{2,1,0:T(4,128)(2,1)}, u32[]{:S(2)}) copy-start(bf16[1,4,4096]{2,1,0:T(4,128)(2,1)} %nv_hbm.1) | copy-start | bytes 98308
  9.4 0.7 %copy-start.7 = (bf16[4,4,512]{2,1,0:T(4,128)(2,1)S(1)}, bf16[4,4,512]{2,1,0:T(4,128)(2,1)}, u32[]{:S(2)}) copy-start(bf16[4,4,512]{2,1,0:T(4,128)(2,1)} %resid_hbm.1) | copy-start | bytes 49156
  10.1 0.7 %copy-start.8 = (s32[4]{0:T(128)S(1)}, s32[4]{0:T(128)}, u32[]{:S(2)}) copy-start(s32[4]{0:T(128)} %tlen.1) | copy-start | bytes 52
  10.8 0.7 %copy-start.9 = (f32[32]{0:T(128)S(1)}, f32[32]{0:T(128)}, u32[]{:S(2)}) copy-start(f32[32]{0:T(128)} %constant.2.clone.slopes) | copy-start | bytes 388

commit v2 on v1

--- a/solution.py
+++ b/solution.py
@@ -236,6 +236,7 @@
     proj_send,
     proj_recv,
     load_sem,
+    cache_sem,
     o_ss,
     o_rs,
     st_ss,
@@ -273,21 +274,41 @@
     def peer(index):
         return {"seq": index // C, "mlp": lax.rem(index, C)}
 
-    loads = [
+    def across(k):
+        return 2 * lax.rem(seq // 2 + k // 2, 2) + lax.rem(lax.rem(seq, 2) + lax.rem(k, 2), 2)
+
+    def partner(k):
+        return across(k // 2) * C + lax.rem(core + lax.rem(k, 2), 2)
+
+    small = [
         pltpu.make_async_copy(q_hbm, q_in, load_sem.at[0]),
         pltpu.make_async_copy(nk_hbm, nk_in, load_sem.at[1]),
         pltpu.make_async_copy(nv_hbm, nv_in, load_sem.at[2]),
-        pltpu.make_async_copy(pk_hbm.at[0], kbuf.at[pl.ds(0, prefix)], load_sem.at[3]),
-        pltpu.make_async_copy(tk_hbm.at[0], kbuf.at[pl.ds(prefix, tail)], load_sem.at[4]),
-        pltpu.make_async_copy(pv_hbm.at[0], vbuf.at[pl.ds(0, prefix)], load_sem.at[5]),
-        pltpu.make_async_copy(tv_hbm.at[0], vbuf.at[pl.ds(prefix, tail)], load_sem.at[6]),
-        pltpu.make_async_copy(resid_hbm, resid_in, load_sem.at[7]),
+        pltpu.make_async_copy(resid_hbm, resid_in, load_sem.at[3]),
     ]
-    wo_load = pltpu.make_async_copy(wo_hbm, wo, load_sem.at[8])
-    wu_load = pltpu.make_async_copy(wu_hbm, wu, load_sem.at[9])
-    wd_load = pltpu.make_async_copy(wd_hbm, wd, load_sem.at[10])
-    for load in loads:
+
+    def cache_loads(k):
+        cols = pl.ds(pl.multiple_of(partner(k) * block, block), block)
+        first, second = pl.ds(0, prefix), pl.ds(prefix, tail)
+        return [
+            pltpu.make_async_copy(pk_hbm.at[0, :, cols], kbuf.at[first, cols], cache_sem.at[0, k]),
+            pltpu.make_async_copy(tk_hbm.at[0, :, cols], kbuf.at[second, cols], cache_sem.at[1, k]),
+            pltpu.make_async_copy(pv_hbm.at[0, :, cols], vbuf.at[first, cols], cache_sem.at[2, k]),
+            pltpu.make_async_copy(tv_hbm.at[0, :, cols], vbuf.at[second, cols], cache_sem.at[3, k]),
+        ]
+
+    wo_load = pltpu.make_async_copy(wo_hbm, wo, load_sem.at[4])
+    wu_load = pltpu.make_async_copy(wu_hbm, wu, load_sem.at[5])
+    wd_load = pltpu.make_async_copy(wd_hbm, wd, load_sem.at[6])
+    for load in small:
         load.start()
+
+    def start_cache(i, carry):
+        for load in cache_loads(N - 1 - i):
+            load.start()
+        return carry
+
+    lax.fori_loop(0, N, start_cache, 0)
 
     barrier = pltpu.get_barrier_semaphore()
     for k in range(1, N):
@@ -331,22 +352,20 @@
     dist[...] = jnp.where(live, apart.astype(F32), FAR)
 
     stage[...] = jnp.zeros_like(stage)
-    loads[1].wait()
+    small[1].wait()
     stage[0:steps, :] = nk_in[0].astype(F32)
     kbuf[prefix + tail : keys, :] = stage[...].astype(BF16)
-    loads[2].wait()
+    small[2].wait()
     stage[0:steps, :] = nv_in[0].astype(F32)
     vbuf[prefix + tail : keys, :] = stage[...].astype(BF16)
-    loads[0].wait()
+    small[0].wait()
     for r in range(group_req):
         stage[r * steps : (r + 1) * steps, :] = q_in[r].astype(F32)
     qbuf[...] = stage[...].astype(BF16)
-    loads[7].wait()
+    small[3].wait()
     for r in range(group_req):
         ybuf[r * steps : (r + 1) * steps, :] = resid_in[r].astype(F32)
 
-    for i in range(3, 7):
-        loads[i].wait()
     wo_load.start()
     wu_load.start()
     wd_load.start()
@@ -357,32 +376,51 @@
     lane = lax.broadcasted_iota(jnp.int32, (rows, LANES), 1)
 
     def partials(i, carry):
-        p = lax.rem(me + 1 + i, N)
-        base = pl.multiple_of(p * block, block)
-        stats = jnp.zeros((rows, LANES), F32)
-        for j in range(heads):
-            cols = pl.ds(base + j * head_dim, head_dim)
-            scores = lax.dot_general(
+        pair = [N - 1 - 2 * i, N - 2 - 2 * i]
+        for k in pair:
+            for load in cache_loads(k):
+                load.wait()
+        places = [(partner(k), j) for k in pair for j in range(heads)]
+        spans = [
+            pl.ds(pl.multiple_of(p * block, block) + j * head_dim, head_dim) for p, j in places
+        ]
+        scores = [
+            lax.dot_general(
                 qbuf[:, cols], kbuf[:, cols], (((1,), (1,)), ((), ())), preferred_element_type=F32
             )
-            scores = scores * inv_scale - slopes[p * heads + j] * dist[...]
-            top = jnp.maximum(jnp.max(scores, axis=1, keepdims=True), FLOOR)
-            weights = jnp.exp(scores - top)
-            total = jnp.sum(weights, axis=1, keepdims=True)
-            mixed = jnp.dot(weights.astype(BF16), vbuf[:, cols], preferred_element_type=F32)
-            o_send[p, :, j * head_dim : (j + 1) * head_dim] = mixed.astype(BF16)
-            stats = jnp.where(lane == j, top, stats)
-            stats = jnp.where(lane == heads + j, total, stats)
-        st_send[p] = stats
-
-        @pl.when(i < N - 1)
-        def _():
-            remote(o_send.at[p], o_recv.at[me], o_ss.at[p], o_rs.at[me], peer(p)).start()
-            remote(st_send.at[p], st_recv.at[me], st_ss.at[p], st_rs.at[me], peer(p)).start()
+            for cols in spans
+        ]
+        scores = [
+            member * inv_scale - slopes[p * heads + j] * dist[...]
+            for member, (p, j) in zip(scores, places)
+        ]
+        tops = [
+            jnp.maximum(jnp.max(member, axis=1, keepdims=True), FLOOR) for member in scores
+        ]
+        weights = [jnp.exp(member - top) for member, top in zip(scores, tops)]
+        totals = [jnp.sum(member, axis=1, keepdims=True) for member in weights]
+        mixed = [
+            jnp.dot(member.astype(BF16), vbuf[:, cols], preferred_element_type=F32)
+            for member, cols in zip(weights, spans)
+        ]
+        for half in range(2):
+            p = places[half * heads][0]
+            stats = jnp.zeros((rows, LANES), F32)
+            for j in range(heads):
+                at = half * heads + j
+                o_send[p, :, j * head_dim : (j + 1) * head_dim] = mixed[at].astype(BF16)
+                stats = jnp.where(lane == j, tops[at], stats)
+                stats = jnp.where(lane == heads + j, totals[at], stats)
+            st_send[p] = stats
+
+            @pl.when(pair[half] > 0)
+            def _():
+                remote(o_send.at[p], o_recv.at[me], o_ss.at[p], o_rs.at[me], peer(p)).start()
+                remote(st_send.at[p], st_recv.at[me], st_ss.at[p], st_rs.at[me], peer(p)).start()
 
         return carry
 
-    lax.fori_loop(0, N, partials, 0)
+    lax.fori_loop(0, N // 2, partials, 0)
     o_recv[me] = o_send[me]
     st_recv[me] = st_send[me]
 
@@ -404,14 +442,14 @@
         for i in range(1, N):
             mixed = mixed + o_recv[i, :, cols].astype(F32) * factors[i][:, j : j + 1]
         att[me, :, cols] = (mixed / whole[:, j : j + 1]).astype(BF16)
-    for k in range(1, N):
-        p = lax.rem(me + k, N)
+    for k in range(N - 1, 0, -1):
+        p = partner(k)
         remote(att.at[me], att.at[me], att_ss.at[p], att_rs.at[me], peer(p)).start()
 
     wo_load.wait()
 
     def out_proj(k, carry):
-        p = lax.rem(me + N - k, N)
+        p = partner(k)
 
         @pl.when(k > 0)
         def _():
@@ -427,8 +465,8 @@
     sums = jnp.where(lane == 0, jnp.sum(y, axis=1, keepdims=True), 0.0)
     sums = jnp.where(lane == 1, jnp.sum(y * y, axis=1, keepdims=True), sums)
     sum_send[...] = sums
-    for k in range(1, N):
-        p = lax.rem(me + k, N)
+    for k in range(N - 1, 0, -1):
+        p = partner(k)
         remote(sum_send, sum_recv.at[me], sum_ss.at[p], sum_rs.at[me], peer(p)).start()
     sum_recv[me] = sums
     for k in range(1, N):
@@ -437,7 +475,7 @@
     sums = jnp.sum(sum_recv[...], axis=0)
     mean = sums[:, 0:1] / width
     var = sums[:, 1:2] / width - mean * mean
-    hidden = (y - mean) * lax.rsqrt(var + 1e-05) * gain_ref[...].astype(F32)
+    hidden = (y - mean) * lax.rsqrt(var + 1e-05) * gain_ref[...].astype(F32)[None, :]
     mine = pl.ds(pl.multiple_of(grp * rows, rows), rows)
     hid[mine, :] = hidden.astype(BF16)
     for k in range(1, G):
@@ -456,7 +494,7 @@
         return jnp.dot(hid[...], wu[:, piece], preferred_element_type=F32)
 
     def pair_blocks(k, carry):
-        z = lax.rem(seq + 1 + k, S)
+        z = across(S - 1 - k)
         up_send[z] = lift(z * C + other).astype(BF16)
         remote(up_send.at[z], up_pair.at[z], pair_ss.at[z], pair_rs.at[z], {"mlp": other}).start()
         return carry
@@ -464,7 +502,7 @@
     lax.fori_loop(0, S, pair_blocks, 0)
 
     def z_blocks(k, carry):
-        z = lax.rem(seq + 1 + k, S)
+        z = across(S - 1 - k)
         part = lift(z * C + core)
         remote(
             up_send.at[z], up_pair.at[z], pair_ss.at[z], pair_rs.at[z], {"mlp": other}
@@ -494,8 +532,8 @@
         lifted = lifted + up_zrecv[z].astype(F32)
     act[me] = (0.5 * lifted * (1.0 + lax.erf(lifted * math.sqrt(0.5)))).astype(BF16)
 
-    for k in range(1, S):
-        z = lax.rem(seq + k, S)
+    for k in range(S - 1, 0, -1):
+        z = across(k)
         remote(act.at[me], act.at[me], act_ss.at[z], act_rs.at[me], {"seq": z}).start()
     remote(act.at[me], act.at[me], fwd_ss.at[seq], act_rs.at[me], {"mlp": other}).start()
 
@@ -508,7 +546,7 @@
     acc[...] = lower(me)
 
     def down(k, carry):
-        z = lax.rem(seq + S - k, S)
+        z = across(k)
         near = z * C + core
         far = z * C + other
 
@@ -633,7 +671,8 @@
             pltpu.VMEM((G * rows, block), F32),
             pltpu.VMEM((G, rows, block), BF16),
             pltpu.VMEM((G, rows, block), BF16),
-            dma((11,)),
+            dma((7,)),
+            dma((4, N)),
             dma((N,)),
             dma((N,)),
             dma((N,)),
@@ -655,7 +694,7 @@
             dma((G,)),
         ],
         compiler_params=pltpu.CompilerParams(
-            collective_id=0, has_side_effects=True, vmem_limit_bytes=44 * 1024 * 1024
+            collective_id=0, has_side_effects=True, vmem_limit_bytes=63 * 1024 * 1024
         ),
         cost_estimate=pl.CostEstimate(
             flops=2 * rows * width * (keys * 2 + block) + 4 * G * rows * block * w_up.shape[1],
@@ -674,7 +713,7 @@
         tail_len,
         slopes,
         resid,
-        ln_gain.reshape(1, block),
+        ln_gain,
         w_out,
         w_up,
         w_down,
@@ -688,7 +727,7 @@
         rows = args[0].shape[0] * args[0].shape[1]
         block = args[9].shape[2]
         lifted = args[12].shape[1] // (S * C)
-        if C == 2 and lifted == block and block % LANES == 0 and rows == NEW_PAD:
+        if (S, C) == (4, 2) and lifted == block and block % LANES == 0 and rows == NEW_PAD:
             return fused(G, S, C, *args)
         return body(*args)
 

time: 64.6 us -> 50.9 us (0.79)
  local copies, waits for them, and re-layouts: 11.4 us -> 1.38 us
  Pallas kernels: 52.1 us -> 48.6 us
    unnamed x21 -> x1, local copies, waits for them, and re-layouts: 10.7 us -> 1.38 us
    pallas_call x1, Pallas kernels: 52.1 us -> 48.6 us  [fused(): pl.pallas_call(functools.partial(layer_kernel, G, S, C), out_shape=jax.Sh...]
    reshape x1 -> x0, local copies, waits for them, and re-layouts: 0.68 us -> none  [fused(): ln_gain.reshape(1, block)]
where the time goes in v2:
time: 50.9 us; the launch traced here: 50.7 us
  Pallas kernels  48.6 us (95%)
  local copies, waits for them, and re-layouts  1.38 us (3%)
  between operations  0.66 us (1%)
    pallas_call x1, Pallas kernels, fused(): pl.pallas_call(functools.partial(layer_kernel, G, S, C), out_shape=jax.Sh...  48.6 us
    unnamed x1, local copies, waits for them, and re-layouts  1.38 us

profile of v2, /device:TPU:0, one launch (start us, length us, event | category | flops | bytes accessed | tf_op | source)
XLA Modules:
  0.0 50.7 jit_solution(7508387273641282615)
XLA Ops:
  0.7 48.6 %shard_map.145 = f32[4,4,512]{2,1,0:T(4,128)} custom-call(bf16[4,4,4096]{2,1,0:T(4,128)(2,1)} %q_hbm.1, bf16[1,4,4096]{2,1,0:T(4,128)(2,1)} %nk_hbm.1, bf16[1,4,4096]{2,1,0:T(4,128)(2,1)} %nv_hbm.1, bf16[1,256,4096]{2,1,0:T(8,128)(2,1)} %pk_hbm.1, bf16[1,256,4096]{2,1,0:T(8,128)(2,1)} %pv_hbm.1, bf16[1,128,4096]{2,1,0:T(8,128)(2,1)} %tk_hbm.1, ...), custom_call_target="tpu_custom_call" | custom-call | flops 708837376 | bytes 19136512 | tf_op jit(solution)/shard_map/pallas_call | solution.py:639
  49.3 1.4 %copy.18 = f32[4,4,512]{2,1,0:T(4,128)} copy(f32[4,4,512]{2,1,0:T(4,128)} %shard_map.145) | data formatting | bytes 65536

commit v3 on v2

--- a/solution.py
+++ b/solution.py
@@ -374,6 +374,17 @@
 
     inv_scale = 1.0 / math.sqrt(head_dim)
     lane = lax.broadcasted_iota(jnp.int32, (rows, LANES), 1)
+    sub = lax.broadcasted_iota(jnp.int32, (rows, LANES), 0)
+
+    def packed(columns):
+        out = jnp.zeros((rows, LANES), F32)
+        for c, column in enumerate(columns):
+            out = jnp.where(lane == sub + c * rows, column, out)
+        return jnp.sum(out, axis=0, keepdims=True)
+
+    def unpacked(line, c):
+        return jnp.sum(jnp.where(lane == sub + c * rows, line, 0.0), axis=1, keepdims=True)
+
 
     def partials(i, carry):
         pair = [N - 1 - 2 * i, N - 2 - 2 * i]
@@ -405,13 +416,11 @@
         ]
         for half in range(2):
             p = places[half * heads][0]
-            stats = jnp.zeros((rows, LANES), F32)
             for j in range(heads):
                 at = half * heads + j
                 o_send[p, :, j * head_dim : (j + 1) * head_dim] = mixed[at].astype(BF16)
-                stats = jnp.where(lane == j, tops[at], stats)
-                stats = jnp.where(lane == heads + j, totals[at], stats)
-            st_send[p] = stats
+            span = slice(half * heads, (half + 1) * heads)
+            st_send[p] = packed(tops[span] + totals[span])
 
             @pl.when(pair[half] > 0)
             def _():
@@ -433,15 +442,19 @@
     for i in range(1, N):
         best = jnp.maximum(best, stats[i])
     factors = [jnp.exp(member - best) for member in stats]
-    whole = factors[0] * pltpu.roll(stats[0], LANES - heads, 1)
+    shift = heads * rows
+    upper = lax.broadcasted_iota(jnp.int32, (1, LANES), 1) >= shift
+    sums_of = [pltpu.roll(member, shift, 1) for member in stats]
+    whole = factors[0] * sums_of[0]
     for i in range(1, N):
-        whole = whole + factors[i] * pltpu.roll(stats[i], LANES - heads, 1)
+        whole = whole + factors[i] * sums_of[i]
+    shares = [jnp.where(upper, 0.0, member / jnp.where(upper, 1.0, whole)) for member in factors]
     for j in range(heads):
         cols = slice(j * head_dim, (j + 1) * head_dim)
-        mixed = o_recv[0, :, cols].astype(F32) * factors[0][:, j : j + 1]
+        mixed = o_recv[0, :, cols].astype(F32) * unpacked(shares[0], j)
         for i in range(1, N):
-            mixed = mixed + o_recv[i, :, cols].astype(F32) * factors[i][:, j : j + 1]
-        att[me, :, cols] = (mixed / whole[:, j : j + 1]).astype(BF16)
+            mixed = mixed + o_recv[i, :, cols].astype(F32) * unpacked(shares[i], j)
+        att[me, :, cols] = mixed.astype(BF16)
     for k in range(N - 1, 0, -1):
         p = partner(k)
         remote(att.at[me], att.at[me], att_ss.at[p], att_rs.at[me], peer(p)).start()
@@ -462,8 +475,7 @@
     lax.fori_loop(0, N, out_proj, 0)
 
     y = ybuf[...]
-    sums = jnp.where(lane == 0, jnp.sum(y, axis=1, keepdims=True), 0.0)
-    sums = jnp.where(lane == 1, jnp.sum(y * y, axis=1, keepdims=True), sums)
+    sums = packed([jnp.sum(y, axis=1, keepdims=True), jnp.sum(y * y, axis=1, keepdims=True)])
     sum_send[...] = sums
     for k in range(N - 1, 0, -1):
         p = partner(k)
@@ -473,8 +485,8 @@
         p = lax.rem(me + N - k, N)
         remote(sum_send, sum_recv.at[p], sum_ss.at[p], sum_rs.at[p], peer(p)).wait_recv()
     sums = jnp.sum(sum_recv[...], axis=0)
-    mean = sums[:, 0:1] / width
-    var = sums[:, 1:2] / width - mean * mean
+    mean = unpacked(sums, 0) / width
+    var = unpacked(sums, 1) / width - mean * mean
     hidden = (y - mean) * lax.rsqrt(var + 1e-05) * gain_ref[...].astype(F32)[None, :]
     mine = pl.ds(pl.multiple_of(grp * rows, rows), rows)
     hid[mine, :] = hidden.astype(BF16)
@@ -656,12 +668,12 @@
             pltpu.VMEM(w_down.shape, BF16),
             pltpu.VMEM((N, rows, block), BF16),
             pltpu.VMEM((N, rows, block), BF16),
-            pltpu.VMEM((N, rows, LANES), F32),
-            pltpu.VMEM((N, rows, LANES), F32),
+            pltpu.VMEM((N, 1, LANES), F32),
+            pltpu.VMEM((N, 1, LANES), F32),
             pltpu.VMEM((N, rows, block), BF16),
             pltpu.VMEM((rows, block), F32),
-            pltpu.VMEM((rows, LANES), F32),
-            pltpu.VMEM((N, rows, LANES), F32),
+            pltpu.VMEM((1, LANES), F32),
+            pltpu.VMEM((N, 1, LANES), F32),
             pltpu.VMEM((G * rows, block), BF16),
             pltpu.VMEM((S, G * rows, lifted), BF16),
             pltpu.VMEM((S, G * rows, lifted), BF16),
@@ -727,7 +739,8 @@
         rows = args[0].shape[0] * args[0].shape[1]
         block = args[9].shape[2]
         lifted = args[12].shape[1] // (S * C)
-        if (S, C) == (4, 2) and lifted == block and block % LANES == 0 and rows == NEW_PAD:
+        heads = block // (args[0].shape[2] // H)
+        if (S, C) == (4, 2) and 2 * heads * rows == LANES and lifted == block and block % LANES == 0 and rows == NEW_PAD:
             return fused(G, S, C, *args)
         return body(*args)
 

time: 50.9 us -> 50 us (0.982)
  Pallas kernels: 48.6 us -> 47.8 us
    pallas_call x1, Pallas kernels: 48.6 us -> 47.8 us  [fused(): pl.pallas_call(functools.partial(layer_kernel, G, S, C), out_shape=jax.Sh...]
where the time goes in v3:
time: 50 us; the launch traced here: 49.8 us
  Pallas kernels  47.8 us (96%)
  local copies, waits for them, and re-layouts  1.38 us (3%)
  between operations  0.66 us (1%)
    pallas_call x1, Pallas kernels, fused(): pl.pallas_call(functools.partial(layer_kernel, G, S, C), out_shape=jax.Sh...  47.8 us
    unnamed x1, local copies, waits for them, and re-layouts  1.38 us

profile of v3, /device:TPU:0, one launch (start us, length us, event | category | flops | bytes accessed | tf_op | source)
XLA Modules:
  0.0 49.8 jit_solution(18076573913751200839)
XLA Ops:
  0.7 47.8 %shard_map.145 = f32[4,4,512]{2,1,0:T(4,128)} custom-call(bf16[4,4,4096]{2,1,0:T(4,128)(2,1)} %q_hbm.1, bf16[1,4,4096]{2,1,0:T(4,128)(2,1)} %nk_hbm.1, bf16[1,4,4096]{2,1,0:T(4,128)(2,1)} %nv_hbm.1, bf16[1,256,4096]{2,1,0:T(8,128)(2,1)} %pk_hbm.1, bf16[1,256,4096]{2,1,0:T(8,128)(2,1)} %pv_hbm.1, bf16[1,128,4096]{2,1,0:T(8,128)(2,1)} %tk_hbm.1, ...), custom_call_target="tpu_custom_call" | custom-call | flops 708837376 | bytes 19136512 | tf_op jit(solution)/shard_map/pallas_call | solution.py:651
  48.4 1.4 %copy.18 = f32[4,4,512]{2,1,0:T(4,128)} copy(f32[4,4,512]{2,1,0:T(4,128)} %shard_map.145) | data formatting | bytes 65536
